TPU v7x, 256 devices: a whole 4x4x8 slice. The times are simulated.
256 devices in a mesh: gz: 32 (over y, z), gy: 8 (over x, core).
Axes of the slice: x: 4, y: 4, z: 8, core: 2. Of those that a mesh axis runs over, the one named last changes fastest.
Arguments:
- fraction: float32 [256, 256, 512], P('gz', 'gy'), may hold values from 0 to 1
- source: float32 [256, 256, 512], P('gz', 'gy'), may hold values from -40 to 40, as said below
- bubble_label: int32 [256, 256, 512], P('gz', 'gy'), may hold values from -1 to 4095, as said below
- subdomain: int32 [256, 256, 512], P('gz', 'gy'), may hold values from 0 to 1023, as said below
- coarse_inverse: float32 [5120, 5120], P(('gz', 'gy')), may hold values from -0.2 to 0.2, as said below
Outputs:
- iterate: float32 [256, 256, 512], P('gz', 'gy')
- residual: float32 [256, 256, 512], P('gz', 'gy')
Inputs may be any that keep to these rules, and one draw needn't show every extreme that they name: `source`: vertical factor 1 + 2 z / 256, so magnitudes grow with depth. `bubble_label`: A cell at plane z and row y carries -1 or the number of a bubble of slab block a and row block y // 32 with |a - z // 8| <= 1; the bubbles of slab block a and row block b are numbered (a 8 + b) * 16 + i with i < 16. Rows y with y % 32 == 0 carry -1. `subdomain`: cells of slab block a and row block b carry (a 8 + b) * 4 + i with i < 4; the number does not change along z and y inside a block and never falls along x. `coarse_inverse`: symmetric positive definite.
All inputs are finite; a program needn't handle non-finite values.
Results may differ from a plain program's by a relative error of at most 0.0003.
Values sent between devices are 32-bit elements; how exact they have to be, the bound alone decides.
A program may use at most 64 MiB of HBM per device.

v0:
```python
from functools import reduce
import jax
import jax.numpy as jnp
from jax import lax
from jax.sharding import PartitionSpec as P

S_DEV = 4
B_DEV = 16
ITERS = 3
surface_tension = 0.5
shift_term = 0.05
gas_drop = 0.75
norm_floor = 0.25
highest = lax.Precision.HIGHEST


def with_halo(block, sides, width):
    for axis, dim in sides:
        count = lax.axis_size(axis)
        forward = [(i, i + 1) for i in range(count - 1)]
        backward = [(target, source) for source, target in forward]
        low = lax.ppermute(
            lax.slice_in_dim(block, block.shape[dim] - width, None, axis=dim), axis, forward
        )
        high = lax.ppermute(lax.slice_in_dim(block, 0, width, axis=dim), axis, backward)
        block = jnp.concatenate([low, block, high], axis=dim)
    return block


def add_all(items):
    return reduce(lambda first, second: first + second, items)


def widen_x(block):
    return jnp.pad(block, [(0, 0)] * (block.ndim - 1) + [(1, 1)])


def six_neighbours(padded):
    return [
        padded[2:, 1:-1, 1:-1],
        padded[:-2, 1:-1, 1:-1],
        padded[1:-1, 2:, 1:-1],
        padded[1:-1, :-2, 1:-1],
        padded[1:-1, 1:-1, 2:],
        padded[1:-1, 1:-1, :-2],
    ]


def normals(padded):
    along = [
        0.5 * (padded[2:, 1:-1, 1:-1] - padded[:-2, 1:-1, 1:-1]),
        0.5 * (padded[1:-1, 2:, 1:-1] - padded[1:-1, :-2, 1:-1]),
        0.5 * (padded[1:-1, 1:-1, 2:] - padded[1:-1, 1:-1, :-2]),
    ]
    length = jnp.maximum(
        jnp.sqrt(along[0] * along[0] + along[1] * along[1] + along[2] * along[2]), norm_floor
    )
    return jnp.stack([member / length for member in along])


def curvature(padded):
    return -(
        0.5 * (padded[0, 2:, 1:-1, 1:-1] - padded[0, :-2, 1:-1, 1:-1])
        + 0.5 * (padded[1, 1:-1, 2:, 1:-1] - padded[1, 1:-1, :-2, 1:-1])
        + 0.5 * (padded[2, 1:-1, 1:-1, 2:] - padded[2, 1:-1, 1:-1, :-2])
    )


def assemble(frac_padded, kappa_padded, source):
    density = 1.0 - gas_drop * frac_padded
    centre = density[1:-1, 1:-1, 1:-1]
    coefs = [2.0 / (centre + other) for other in six_neighbours(density)]
    fraction = frac_padded[1:-1, 1:-1, 1:-1]
    kappa = kappa_padded[1:-1, 1:-1, 1:-1]
    terms = [
        coef * (0.5 * (kappa + kappa_other)) * (frac_other - fraction)
        for coef, frac_other, kappa_other in zip(
            coefs, six_neighbours(frac_padded), six_neighbours(kappa_padded)
        )
    ]
    rhs = source - surface_tension * add_all(terms)
    diagonal = shift_term + add_all(coefs)
    return (coefs, diagonal, rhs)


def operate_padded(padded, coefs, diagonal):
    return diagonal * padded[1:-1, 1:-1, 1:-1] - add_all(
        [coef * other for coef, other in zip(coefs, six_neighbours(padded))]
    )


def factor_planes(diagonal_planes, down_planes):
    inverse = [1.0 / diagonal_planes[0]]
    mults = [None]
    for level in range(1, len(diagonal_planes)):
        mult = down_planes[level] * inverse[level - 1]
        inverse.append(1.0 / (diagonal_planes[level] - mult * down_planes[level]))
        mults.append(mult)
    return (inverse, mults)


def solve_planes(values, inverse, mults, up_planes):
    count = len(values)
    forward = [values[0]]
    for level in range(1, count):
        forward.append(values[level] + mults[level] * forward[level - 1])
    result = [forward[count - 1] * inverse[count - 1]]
    for level in range(count - 2, -1, -1):
        result.insert(0, (forward[level] + up_planes[level] * result[0]) * inverse[level])
    return result


def region_sums(field, flat_bins, slots):
    flat_field = field.reshape(field.shape[0], -1)

    def one_plane(pair):
        plane_bins, plane_values = pair
        onehot = (plane_bins[None, :] == slots[:, None]).astype(jnp.float32)
        return jnp.dot(onehot, plane_values, precision=highest)

    return jnp.sum(lax.map(one_plane, (flat_bins, flat_field)), axis=0)


def region_values(window, flat_bins, slots):

    def one_plane(plane_bins):
        onehot = (plane_bins[None, :] == slots[:, None]).astype(jnp.float32)
        return jnp.dot(window, onehot, precision=highest)

    return lax.map(one_plane, flat_bins)


def on_device(fraction, source, bubble_label, subdomain, coarse_inverse):
    planes = fraction.shape[0]
    slabs = lax.axis_size("gz")
    columns = lax.axis_size("gy")
    slab_index = lax.axis_index("gz")
    column_index = lax.axis_index("gy")
    devices = slabs * columns
    here = slab_index * columns + column_index
    frac_padded = widen_x(with_halo(fraction, (("gz", 0), ("gy", 1)), 1))
    normal = normals(frac_padded)
    normal_padded = widen_x(with_halo(normal, (("gz", 1), ("gy", 2)), 1))
    kappa = curvature(normal_padded)
    kappa_padded = widen_x(with_halo(kappa, (("gz", 0), ("gy", 1)), 1))
    coefs, diagonal, rhs = assemble(frac_padded, kappa_padded, source)
    inverse, mults = factor_planes(
        [diagonal[level] for level in range(planes)], [coefs[1][level] for level in range(planes)]
    )
    up_planes = [coefs[0][level] for level in range(planes)]
    owner_slab = bubble_label // B_DEV // columns
    bubble_bin = S_DEV + (owner_slab - slab_index + 1) * B_DEV + bubble_label % B_DEV
    bins = jnp.where(bubble_label >= 0, bubble_bin, subdomain - here * S_DEV)
    flat_bins = bins.reshape(planes, -1)
    slots = jnp.arange(S_DEV + 3 * B_DEV, dtype=jnp.int32)
    device_rows = jnp.arange(devices, dtype=jnp.int32)[:, None]
    blank = jnp.zeros((S_DEV,), jnp.float32)

    def precondition(residual):
        block = jnp.stack(
            solve_planes([residual[level] for level in range(planes)], inverse, mults, up_planes)
        )
        partial_value = region_sums(residual, flat_bins, slots)
        own_row = jnp.concatenate(
            [partial_value[:S_DEV], partial_value[S_DEV + B_DEV : S_DEV + 2 * B_DEV]]
        )
        below_row = jnp.concatenate([blank, partial_value[S_DEV : S_DEV + B_DEV]])
        above_row = jnp.concatenate([blank, partial_value[S_DEV + 2 * B_DEV :]])
        spread = (
            jnp.where(device_rows == here, own_row, 0.0)
            + jnp.where(device_rows == here - columns, below_row, 0.0)
            + jnp.where(device_rows == here + columns, above_row, 0.0)
        ).reshape(-1)
        totals = lax.psum(spread, ("gz", "gy"))
        coarse_own = jnp.dot(coarse_inverse, totals, precision=highest)
        bubble_rows = with_halo(coarse_own[S_DEV:][None, :], (("gz", 0),), 1)
        window = jnp.concatenate(
            [coarse_own[:S_DEV], bubble_rows[0], coarse_own[S_DEV:], bubble_rows[2]]
        )
        correction = region_values(window, flat_bins, slots).reshape(residual.shape)
        direction = block + correction
        product = lax.psum(jnp.sum(residual * direction), ("gz", "gy"))
        return (direction, product)

    iterate = jnp.zeros_like(rhs)
    residual = rhs
    direction, product = precondition(residual)
    search = direction
    for sweep in range(ITERS):
        padded = widen_x(with_halo(search, (("gz", 0), ("gy", 1)), 1))
        image = operate_padded(padded, coefs, diagonal)
        alpha = product / lax.psum(jnp.sum(search * image), ("gz", "gy"))
        iterate = iterate + alpha * search
        residual = residual - alpha * image
        if sweep + 1 < ITERS:
            direction, fresh = precondition(residual)
            search = direction + fresh / product * search
            product = fresh
    return (iterate, residual)


def solution(mesh):
    placed = (
        P("gz", "gy", None),
        P("gz", "gy", None),
        P("gz", "gy", None),
        P("gz", "gy", None),
        P(("gz", "gy"), None),
    )
    return jax.shard_map(
        on_device,
        mesh=mesh,
        in_specs=placed,
        out_specs=(P("gz", "gy", None), P("gz", "gy", None)),
        check_vma=False,
    )
```

profile of v0, /device:TPU:1, one launch (start us, length us, event | category | flops | bytes accessed | tf_op | source)
XLA Modules:
  0.0 992.9 jit_solution(13966434582722056104)
XLA Ops:
  1.6 4.4 collective-permute-start
  11.3 4.9 collective-permute-start.2
  18.1 3.2 collective-permute-done.3
  25.9 4.2 collective-permute-start.5
  36.5 3.9 collective-permute-start.7
  40.4 2.9 fusion.39
  44.5 4.6 select_maximum_fusion
  51.7 5.1 collective-permute-start.9
  60.0 3.6 collective-permute-start.11
  66.3 7.0 fusion.75
  74.4 32.1 %while.66 = (s32[]{:T(128)}, f32[8,52]{1,0:T(8,128)S(1)}, s32[8,16384]{1,0:T(8,128)}, f32[8,16384]{1,0:T(8,128)}, s32[]{:T(128)}, /*index=5*/s32[]{:T(128)}) while((s32[]{:T(128)}, f32[8,52]{1,0:T(8,128)S(1)}, s32[8,16384]{1,0:T(8,128)}, f32[8,16384]{1,0:T(8,128)}, s32[]{:T(128)}, /*index=5*/s32[]{:T(128)}) %tuple.202), condition=%wide.region_1.2_spmd.clone, body=%wide.region_0.1_spmd.clone.sunk | while | flops 11075586 | bytes 263357 | solution.py:121
  75.6 2.9 fusion.170
  79.6 2.9 fusion.170
  83.6 2.9 fusion.170
  87.6 2.9 fusion.170
  91.6 2.9 fusion.170
  99.6 2.9 fusion.170
  103.6 2.9 fusion.170
  107.1 85.8 %psum.63 = f32[5120]{0:T(1024)S(1)} all-reduce(f32[5120]{0:T(1024)S(1)} %add.709), channel_id=1, replica_groups=mesh['gz'=32,'gy'=8] {'gz','gy'}, use_global_device_ids=true, to_apply=%region_3.4 | all-reduce | flops 5120 | bytes 40960 | tf_op jit(solution)/shard_map/psum | solution.py:174
  194.8 4.5 collective-permute-start.12
  203.7 23.2 %while.67 = (s32[]{:T(128)}, f32[8,16384]{1,0:T(8,128)S(1)}, s32[8,16384]{1,0:T(8,128)}, f32[52]{0:T(128)S(1)}, s32[]{:T(128)}, /*index=5*/s32[]{:T(128)}) while((s32[]{:T(128)}, f32[8,16384]{1,0:T(8,128)S(1)}, s32[8,16384]{1,0:T(8,128)}, f32[52]{0:T(128)S(1)}, s32[]{:T(128)}, /*index=5*/s32[]{:T(128)}) %tuple.197), condition=%wide.region_5.6_spmd.clone, body=%wide.region_4.5_spmd.clone.sunk | while | flops 11075586 | bytes 393501 | solution.py:130
  230.5 4.0 collective-permute-start.15
  235.9 4.0 collective-permute-start.16
  243.8 3.6 multiply_reduce_fusion.4
  247.4 80.5 %all-reduce.12 = (f32[]{:T(128)}, f32[]{:T(128)}) all-reduce(f32[]{:T(128)} %get-tuple-element.231, f32[]{:T(128)} %get-tuple-element.230), channel_id=1, replica_groups=mesh['gz'=32,'gy'=8] {'gz','gy'}, use_global_device_ids=true, to_apply=%region_7.8 | all-reduce | flops 2 | bytes 16 | tf_op jit(solution)/shard_map/psum | solution.py:182
  333.3 32.1 %while.68 = (s32[]{:T(128)}, f32[8,52]{1,0:T(8,128)S(1)}, s32[8,16384]{1,0:T(8,128)}, f32[8,16384]{1,0:T(8,128)}, s32[]{:T(128)}, /*index=5*/s32[]{:T(128)}) while((s32[]{:T(128)}, f32[8,52]{1,0:T(8,128)S(1)}, s32[8,16384]{1,0:T(8,128)}, f32[8,16384]{1,0:T(8,128)}, s32[]{:T(128)}, /*index=5*/s32[]{:T(128)}) %tuple.203), condition=%wide.region_11.12_spmd.clone, body=%wide.region_10.11_spmd.clone.sunk | while | flops 11075586 | bytes 263357 | solution.py:121
  334.4 2.9 fusion.173
  346.4 2.9 fusion.173
  350.5 2.9 fusion.173
  362.5 2.9 fusion.173
  366.0 73.9 %psum.66 = f32[5120]{0:T(1024)S(1)} all-reduce(f32[5120]{0:T(1024)S(1)} %add.732), channel_id=1, replica_groups=mesh['gz'=32,'gy'=8] {'gz','gy'}, use_global_device_ids=true, to_apply=%region_13.14 | all-reduce | flops 5120 | bytes 40960 | tf_op jit(solution)/shard_map/psum | solution.py:174
  448.7 23.2 %while.69 = (s32[]{:T(128)}, f32[8,16384]{1,0:T(8,128)S(1)}, s32[8,16384]{1,0:T(8,128)}, f32[52]{0:T(128)S(1)}, s32[]{:T(128)}, /*index=5*/s32[]{:T(128)}) while((s32[]{:T(128)}, f32[8,16384]{1,0:T(8,128)S(1)}, s32[8,16384]{1,0:T(8,128)}, f32[52]{0:T(128)S(1)}, s32[]{:T(128)}, /*index=5*/s32[]{:T(128)}) %tuple.199), condition=%wide.region_15.16_spmd.clone, body=%wide.region_14.15_spmd.clone.sunk | while | flops 11075586 | bytes 393501 | solution.py:130
  474.3 76.8 %psum.67 = f32[]{:T(128)} all-reduce(f32[]{:T(128)} %multiply_reduce_fusion.3), channel_id=1, replica_groups=mesh['gz'=32,'gy'=8] {'gz','gy'}, use_global_device_ids=true, to_apply=%region_17.18 | all-reduce | flops 1 | bytes 8 | tf_op jit(solution)/shard_map/psum | solution.py:182
  555.5 4.3 collective-permute-start.21
  561.8 3.4 collective-permute-start.22
  570.0 3.4 multiply_reduce_fusion.2
  573.4 78.3 %psum.68 = f32[]{:T(128)} all-reduce(f32[]{:T(128)} %get-tuple-element.294), channel_id=1, replica_groups=mesh['gz'=32,'gy'=8] {'gz','gy'}, use_global_device_ids=true, to_apply=%region_19.20 | all-reduce | flops 1 | bytes 8 | tf_op jit(solution)/shard_map/psum | solution.py:192
  655.3 32.0 %while.70 = (s32[]{:T(128)}, f32[8,52]{1,0:T(8,128)S(1)}, s32[8,16384]{1,0:T(8,128)}, f32[8,16384]{1,0:T(8,128)}, s32[]{:T(128)}, /*index=5*/s32[]{:T(128)}) while((s32[]{:T(128)}, f32[8,52]{1,0:T(8,128)S(1)}, s32[8,16384]{1,0:T(8,128)}, f32[8,16384]{1,0:T(8,128)}, s32[]{:T(128)}, /*index=5*/s32[]{:T(128)}) %tuple.204), condition=%wide.region_21.22_spmd.clone, body=%wide.region_20.21_spmd.clone.sunk | while | flops 11075586 | bytes 263357 | solution.py:121
  656.4 2.9 fusion.176
  668.4 2.9 fusion.176
  680.4 2.9 fusion.176
  684.4 2.9 fusion.176
  689.5 73.9 %psum.69 = f32[5120]{0:T(1024)S(1)} all-reduce(f32[5120]{0:T(1024)S(1)} %add.757), channel_id=1, replica_groups=mesh['gz'=32,'gy'=8] {'gz','gy'}, use_global_device_ids=true, to_apply=%region_23.24 | all-reduce | flops 5120 | bytes 40960 | tf_op jit(solution)/shard_map/psum | solution.py:174
  776.2 34.6 %while.71 = (s32[]{:T(128)}, f32[8,16384]{1,0:T(8,128)}, s32[8,16384]{1,0:T(8,128)}, f32[52]{0:T(128)S(1)}, s32[]{:T(128)}, /*index=5*/s32[]{:T(128)}) while((s32[]{:T(128)}, f32[8,16384]{1,0:T(8,128)}, s32[8,16384]{1,0:T(8,128)}, f32[52]{0:T(128)S(1)}, s32[]{:T(128)}, /*index=5*/s32[]{:T(128)}) %tuple.201), condition=%wide.region_25.26_spmd.clone, body=%wide.region_24.25_spmd.clone.sunk | while | flops 11075586 | bytes 393501 | solution.py:130
  812.9 76.7 %psum.70 = f32[]{:T(128)} all-reduce(f32[]{:T(128)} %multiply_reduce_fusion.1), channel_id=1, replica_groups=mesh['gz'=32,'gy'=8] {'gz','gy'}, use_global_device_ids=true, to_apply=%region_27.28 | all-reduce | flops 1 | bytes 8 | tf_op jit(solution)/shard_map/psum | solution.py:182
  894.1 4.3 collective-permute-start.27
  899.7 3.4 collective-permute-start.28
  909.0 78.3 %psum.71 = f32[]{:T(128)} all-reduce(f32[]{:T(128)} %get-tuple-element.282), channel_id=1, replica_groups=mesh['gz'=32,'gy'=8] {'gz','gy'}, use_global_device_ids=true, to_apply=%region_29.30 | all-reduce | flops 1 | bytes 8 | tf_op jit(solution)/shard_map/psum | solution.py:192
  (358 shorter events, 237.7 us)
Async XLA Ops:
  0.6 192.3 %copy-start = (f32[20,5120]{1,0:T(8,128)S(1)}, f32[20,5120]{1,0:T(8,128)}, u32[]{:S(2)}) copy-start(f32[20,5120]{1,0:T(8,128)} %param.21) | copy-start | bytes 1228804
  0.6 21.1 %copy-start.13 = (f32[8,32,512]{2,1,0:T(8,128)S(1)}, f32[8,32,512]{2,1,0:T(8,128)}, u32[]{:S(2)}) copy-start(f32[8,32,512]{2,1,0:T(8,128)} %param.17) | copy-start | bytes 1572868
  1.6 5.7 collective-permute-start
  6.0 5.2 collective-permute-start.1
  11.3 6.9 collective-permute-start.2
  16.2 5.1 collective-permute-start.3
  24.5 20.0 %copy-start.4 = (f32[1,8,32,512]{3,2,1,0:T(8,128)S(1)}, f32[1,8,32,512]{3,2,1,0:T(8,128)}, u32[]{:S(2)}) copy-start(f32[1,8,32,512]{3,2,1,0:T(8,128)} %copy-done.3) | copy-start | bytes 1572868
  24.5 7.1 collective-permute-start.4
  25.9 7.4 collective-permute-start.5
  34.6 8.7 collective-permute-start.6
  36.5 6.8 collective-permute-start.7
  50.2 6.5 collective-permute-start.8
  51.7 6.4 collective-permute-start.9
  58.1 7.8 collective-permute-start.10
  60.0 5.8 collective-permute-start.11
  63.7 43.1 %copy-start.37 = (pred[256]{0:T(512)(128)(4,1)}, pred[256]{0:T(512)(128)(4,1)S(1)}, u32[]{:S(2)}) copy-start(pred[256]{0:T(512)(128)(4,1)S(1)} %iota_compare_fusion.18) | copy-start | bytes 772
  74.4 124.9 %copy-start.5 = (f32[8,32,512]{2,1,0:T(8,128)S(1)}, f32[8,32,512]{2,1,0:T(8,128)}, u32[]{:S(2)}) copy-start(f32[8,32,512]{2,1,0:T(8,128)} %get-tuple-element.334) | copy-start | bytes 1572868
  193.5 9.3 collective-permute-start.13
  194.8 8.0 collective-permute-start.12
  201.8 242.8 %copy-start.18 = (f32[1,32,512]{2,1,0:T(8,128)}, f32[1,32,512]{2,1,0:T(8,128)S(1)}, u32[]{:S(2)}) copy-start(f32[1,32,512]{2,1,0:T(8,128)S(1)} %get-tuple-element.325) | copy-start | bytes 196612
  202.6 242.9 %copy-start.22 = (f32[1,32,512]{2,1,0:T(8,128)}, f32[1,32,512]{2,1,0:T(8,128)S(1)}, u32[]{:S(2)}) copy-start(f32[1,32,512]{2,1,0:T(8,128)S(1)} %get-tuple-element.316) | copy-start | bytes 196612
  202.7 242.9 %copy-start.23 = (f32[1,32,512]{2,1,0:T(8,128)}, f32[1,32,512]{2,1,0:T(8,128)S(1)}, u32[]{:S(2)}) copy-start(f32[1,32,512]{2,1,0:T(8,128)S(1)} %get-tuple-element.319) | copy-start | bytes 196612
  202.7 243.0 %copy-start.24 = (f32[1,32,512]{2,1,0:T(8,128)}, f32[1,32,512]{2,1,0:T(8,128)S(1)}, u32[]{:S(2)}) copy-start(f32[1,32,512]{2,1,0:T(8,128)S(1)} %get-tuple-element.320) | copy-start | bytes 196612
  202.7 243.0 %copy-start.25 = (f32[1,32,512]{2,1,0:T(8,128)}, f32[1,32,512]{2,1,0:T(8,128)S(1)}, u32[]{:S(2)}) copy-start(f32[1,32,512]{2,1,0:T(8,128)S(1)} %get-tuple-element.321) | copy-start | bytes 196612
  229.2 5.3 collective-permute-start.14
  230.5 5.3 collective-permute-start.15
  235.9 6.6 collective-permute-start.16
  239.9 3.5 collective-permute-start.17
  333.3 32.4 %copy-start.38 = (pred[256]{0:T(512)(128)(4,1)S(1)}, pred[256]{0:T(512)(128)(4,1)}, u32[]{:S(2)}) copy-start(pred[256]{0:T(512)(128)(4,1)} %copy-done.37) | copy-start | bytes 772
  333.3 111.3 %copy-start.28 = (f32[1,32,512]{2,1,0:T(8,128)S(1)}, f32[1,32,512]{2,1,0:T(8,128)}, u32[]{:S(2)}) copy-start(f32[1,32,512]{2,1,0:T(8,128)} %get-tuple-element.330) | copy-start | bytes 196612
  333.3 112.4 %copy-start.26 = (f32[1,32,512]{2,1,0:T(8,128)S(1)}, f32[1,32,512]{2,1,0:T(8,128)}, u32[]{:S(2)}) copy-start(f32[1,32,512]{2,1,0:T(8,128)} %get-tuple-element.322) | copy-start | bytes 196612
  333.3 112.4 %copy-start.27 = (f32[1,32,512]{2,1,0:T(8,128)S(1)}, f32[1,32,512]{2,1,0:T(8,128)}, u32[]{:S(2)}) copy-start(f32[1,32,512]{2,1,0:T(8,128)} %get-tuple-element.323) | copy-start | bytes 196612
  440.5 7.4 collective-permute-start.18
  443.3 4.6 collective-permute-start.19
  471.9 79.3 %copy-start.14 = (f32[8,16384]{1,0:T(8,128)}, f32[8,16384]{1,0:T(8,128)S(1)}, u32[]{:S(2)}) copy-start(f32[8,16384]{1,0:T(8,128)S(1)} %get-tuple-element.167) | copy-start | bytes 1572868
  471.9 98.1 %copy-start.6 = (f32[8,32,512]{2,1,0:T(8,128)S(1)}, f32[8,32,512]{2,1,0:T(8,128)}, u32[]{:S(2)}) copy-start(f32[8,32,512]{2,1,0:T(8,128)} %get-tuple-element.334) | copy-start | bytes 1572868
  554.2 5.6 collective-permute-start.20
  555.5 5.6 collective-permute-start.21
  561.8 5.8 collective-permute-start.22
  565.2 3.5 collective-permute-start.23
  655.3 32.3 %copy-start.39 = (pred[256]{0:T(512)(128)(4,1)S(1)}, pred[256]{0:T(512)(128)(4,1)}, u32[]{:S(2)}) copy-start(pred[256]{0:T(512)(128)(4,1)} %copy-done.37) | copy-start | bytes 772
  764.0 11.3 %collective-permute-start.24 = (f32[1,16]{1,0:T(1,128)S(1)}, f32[1,16]{1,0:T(1,128)S(1)}, u32[]{:S(2)}, u32[]{:S(2)}) collective-permute-start(f32[1,16]{1,0:T(1,128)S(1)} %get-tuple-element.369), channel_id=1, source_target_pairs={{0,8},{8,16},{16,24},{24,32},{32,40},{40,48},{48,56},{56,64},{64,7... | collective-permute-start | bytes 200 | tf_op jit(solution)/shard_map/ppermute | solution.py:22
  766.8 8.5 collective-permute-start.25
  892.7 16.2 %copy-start.2 = (f32[8,32,512]{2,1,0:T(8,128)}, f32[8,32,512]{2,1,0:T(8,128)S(1)}, u32[]{:S(2)}) copy-start(f32[8,32,512]{2,1,0:T(8,128)S(1)} %multiply_add_fusion.1) | copy-start | bytes 1572868
  892.8 5.6 collective-permute-start.26
  894.1 5.6 collective-permute-start.27
  899.7 5.8 collective-permute-start.28
  903.1 3.3 collective-permute-start.29
  (22 other events, 165.6 us)
where the time goes:
time: 1010 us; the launch traced here: 993 us
  blocking collectives  624 us (62%)
  matrix products  101 us (10%)
  local copies, waits for them, and re-layouts  95.5 us (9%)
  starting transfers between devices  84.6 us (8%)
  other arithmetic  60.3 us (6%)
  waiting for transfers between devices  17.2 us (2%)
    psum x3, blocking collectives, precondition(): product = lax.psum(jnp.sum(residual * direction), ('gz', 'gy'))  234 us
    psum x3, blocking collectives, precondition(): totals = lax.psum(spread, ('gz', 'gy'))  234 us
    psum x2, blocking collectives, on_device(): alpha = product / lax.psum(jnp.sum(search * image), ('gz', 'gy'))  157 us
    dot_general x24, matrix products, one_plane(): return jnp.dot(onehot, plane_values, precision=highest)  68.5 us
    ppermute x15, starting transfers between devices, with_halo(): lax.ppermute(lax.slice_in_dim(block, block.shape[dim] - width, None, axis...  56.1 us
    dynamic_slice x48, local copies, waits for them, and re-layouts, region_sums(): return jnp.sum(lax.map(one_plane, (flat_bins, flat_field)), axis=0)  52.5 us
    dot_general x24, matrix products, one_plane(): return jnp.dot(window, onehot, precision=highest)  31.3 us
    ppermute x15, starting transfers between devices, with_halo(): lax.ppermute(lax.slice_in_dim(block, 0, width, axis=dim), axis, backward)  28.5 us
  transfers between devices with their start and end apart: 30, of which 11 were waited for; matrix products, arithmetic and copies ran while one was open for 2% of the time, Pallas kernels for 0%

commit v1 on v0

--- a/solution.py
+++ b/solution.py
@@ -171,7 +171,7 @@
             + jnp.where(device_rows == here - columns, below_row, 0.0)
             + jnp.where(device_rows == here + columns, above_row, 0.0)
         ).reshape(-1)
-        totals = lax.psum(spread, ("gz", "gy"))
+        totals = jnp.sum(lax.all_gather(spread, ("gz", "gy")), axis=0)
         coarse_own = jnp.dot(coarse_inverse, totals, precision=highest)
         bubble_rows = with_halo(coarse_own[S_DEV:][None, :], (("gz", 0),), 1)
         window = jnp.concatenate(

time: 1010 us -> 1140 us (1.13)
  waiting for transfers between devices: 17.2 us -> 351 us
  blocking collectives: 624 us -> 388 us
  other arithmetic: 60.3 us -> 77.3 us
  between operations: 8.69 us -> 21.5 us
    all_gather x0 -> x3, waiting for transfers between devices: none -> 326 us  [precondition(): totals = jnp.sum(lax.all_gather(spread, ('gz', 'gy')), axis=0)]
    psum x3 -> x0, blocking collectives: 234 us -> none  [precondition(): totals = lax.psum(spread, ('gz', 'gy'))]
    reduce_sum x0 -> x3, other arithmetic: none -> 15.9 us  [precondition(): totals = jnp.sum(lax.all_gather(spread, ('gz', 'gy')), axis=0)]
  transfers between devices with their start and end apart: 30 -> 33, of which waited for: 11 -> 17; matrix products, arithmetic and copies ran while one was open for 2% -> 2% of each run, Pallas kernels for 0% -> 0%
where the time goes in v1:
time: 1140 us; the launch traced here: 1120 us
  blocking collectives  388 us (34%)
  waiting for transfers between devices  351 us (31%)
  matrix products  101 us (9%)
  local copies, waits for them, and re-layouts  97.4 us (9%)
  starting transfers between devices  84 us (7%)
  other arithmetic  77.3 us (7%)
  between operations  21.5 us (2%)
    all_gather x3, waiting for transfers between devices, precondition(): totals = jnp.sum(lax.all_gather(spread, ('gz', 'gy')), axis=0)  326 us
    psum x3, blocking collectives, precondition(): product = lax.psum(jnp.sum(residual * direction), ('gz', 'gy'))  236 us
    psum x2, blocking collectives, on_device(): alpha = product / lax.psum(jnp.sum(search * image), ('gz', 'gy'))  152 us
    dot_general x24, matrix products, one_plane(): return jnp.dot(onehot, plane_values, precision=highest)  68.5 us
    ppermute x15, starting transfers between devices, with_halo(): lax.ppermute(lax.slice_in_dim(block, block.shape[dim] - width, None, axis...  53.8 us
    dynamic_slice x48, local copies, waits for them, and re-layouts, region_sums(): return jnp.sum(lax.map(one_plane, (flat_bins, flat_field)), axis=0)  52.5 us
    dot_general x24, matrix products, one_plane(): return jnp.dot(window, onehot, precision=highest)  31.3 us
    ppermute x15, starting transfers between devices, with_halo(): lax.ppermute(lax.slice_in_dim(block, 0, width, axis=dim), axis, backward)  29.4 us
  transfers between devices with their start and end apart: 33, of which 17 were waited for; matrix products, arithmetic and copies ran while one was open for 2% of the time, Pallas kernels for 0%

profile of v1, /device:TPU:1, one launch (start us, length us, event | category | flops | bytes accessed | tf_op | source)
XLA Modules:
  0.0 1122.5 jit_solution(1653831584007991762)
XLA Ops:
  8.2 4.4 collective-permute-start
  17.9 4.9 collective-permute-start.2
  24.7 3.2 collective-permute-done.3
  31.4 4.2 collective-permute-start.5
  41.9 3.9 collective-permute-start.7
  45.7 2.9 fusion.39
  48.6 4.4 select_maximum_fusion
  55.7 5.1 collective-permute-start.9
  64.4 3.7 collective-permute-start.11
  70.8 7.1 fusion.75
  79.1 32.1 %while.66 = (s32[]{:T(128)}, f32[8,52]{1,0:T(8,128)S(1)}, s32[8,16384]{1,0:T(8,128)}, f32[8,16384]{1,0:T(8,128)}, s32[]{:T(128)}, /*index=5*/s32[]{:T(128)}) while((s32[]{:T(128)}, f32[8,52]{1,0:T(8,128)S(1)}, s32[8,16384]{1,0:T(8,128)}, f32[8,16384]{1,0:T(8,128)}, s32[]{:T(128)}, /*index=5*/s32[]{:T(128)}) %tuple.208), condition=%wide.region_1.2_spmd.clone, body=%wide.region_0.1_spmd.clone.sunk | while | flops 11075586 | bytes 263357 | solution.py:121
  84.2 2.9 fusion.170
  88.2 2.9 fusion.170
  100.2 2.9 fusion.170
  104.2 2.9 fusion.170
  116.5 120.8 %all-gather.7.cloned.1.call-done = f32[256,1,5120]{2,1,0:T(1,128)} async-done(((f32[1,1,5120]{2,1,0:T(1,128)}), f32[256,1,5120]{2,1,0:T(1,128)}) %all-gather.7.cloned.1.call-update) | async-done | bytes 5242896 | tf_op jit(solution)/shard_map/all_gather | solution.py:174
  237.3 5.3 reduce_sum.109
  244.5 4.0 collective-permute-start.12
  249.3 23.2 %while.67 = (s32[]{:T(128)}, f32[8,16384]{1,0:T(8,128)S(1)}, s32[8,16384]{1,0:T(8,128)}, f32[52]{0:T(128)S(1)}, s32[]{:T(128)}, /*index=5*/s32[]{:T(128)}) while((s32[]{:T(128)}, f32[8,16384]{1,0:T(8,128)S(1)}, s32[8,16384]{1,0:T(8,128)}, f32[52]{0:T(128)S(1)}, s32[]{:T(128)}, /*index=5*/s32[]{:T(128)}) %tuple.203), condition=%wide.region_5.6_spmd.clone, body=%wide.region_4.5_spmd.clone.sunk | while | flops 11075586 | bytes 393501 | solution.py:130
  276.2 4.2 collective-permute-start.15
  281.7 4.4 collective-permute-start.16
  286.2 3.1 collective-permute-start.17
  290.6 3.6 multiply_reduce_fusion.4
  294.2 80.1 %all-reduce.12 = (f32[]{:T(128)}, f32[]{:T(128)}) all-reduce(f32[]{:T(128)} %get-tuple-element.231, f32[]{:T(128)} %get-tuple-element.230), channel_id=1, replica_groups=mesh['gz'=32,'gy'=8] {'gz','gy'}, use_global_device_ids=true, to_apply=%region_7.8 | all-reduce | flops 2 | bytes 16 | tf_op jit(solution)/shard_map/psum | solution.py:182
  379.7 32.1 %while.68 = (s32[]{:T(128)}, f32[8,52]{1,0:T(8,128)S(1)}, s32[8,16384]{1,0:T(8,128)}, f32[8,16384]{1,0:T(8,128)}, s32[]{:T(128)}, /*index=5*/s32[]{:T(128)}) while((s32[]{:T(128)}, f32[8,52]{1,0:T(8,128)S(1)}, s32[8,16384]{1,0:T(8,128)}, f32[8,16384]{1,0:T(8,128)}, s32[]{:T(128)}, /*index=5*/s32[]{:T(128)}) %tuple.209), condition=%wide.region_11.12_spmd.clone, body=%wide.region_10.11_spmd.clone.sunk | while | flops 11075586 | bytes 263357 | solution.py:121
  388.8 2.9 fusion.173
  392.8 2.9 fusion.173
  404.9 2.9 fusion.173
  408.9 2.9 fusion.173
  421.4 102.3 %all-gather.9.cloned.1.call-done = f32[256,1,5120]{2,1,0:T(1,128)} async-done(((f32[1,1,5120]{2,1,0:T(1,128)}), f32[256,1,5120]{2,1,0:T(1,128)}) %all-gather.9.cloned.1.call-update) | async-done | bytes 5242896 | tf_op jit(solution)/shard_map/all_gather | solution.py:174
  523.7 5.3 reduce_sum.113
  533.2 3.0 collective-permute-done.19
  536.3 23.2 %while.69 = (s32[]{:T(128)}, f32[8,16384]{1,0:T(8,128)S(1)}, s32[8,16384]{1,0:T(8,128)}, f32[52]{0:T(128)S(1)}, s32[]{:T(128)}, /*index=5*/s32[]{:T(128)}) while((s32[]{:T(128)}, f32[8,16384]{1,0:T(8,128)S(1)}, s32[8,16384]{1,0:T(8,128)}, f32[52]{0:T(128)S(1)}, s32[]{:T(128)}, /*index=5*/s32[]{:T(128)}) %tuple.205), condition=%wide.region_15.16_spmd.clone, body=%wide.region_14.15_spmd.clone.sunk | while | flops 11075586 | bytes 393501 | solution.py:130
  561.9 78.0 %psum.44 = f32[]{:T(128)} all-reduce(f32[]{:T(128)} %multiply_reduce_fusion.3), channel_id=1, replica_groups=mesh['gz'=32,'gy'=8] {'gz','gy'}, use_global_device_ids=true, to_apply=%region_17.18 | all-reduce | flops 1 | bytes 8 | tf_op jit(solution)/shard_map/psum | solution.py:182
  644.2 4.0 collective-permute-start.21
  650.1 3.7 collective-permute-start.22
  658.5 3.4 multiply_reduce_fusion.2
  661.8 76.2 %psum.45 = f32[]{:T(128)} all-reduce(f32[]{:T(128)} %get-tuple-element.294), channel_id=1, replica_groups=mesh['gz'=32,'gy'=8] {'gz','gy'}, use_global_device_ids=true, to_apply=%region_19.20 | all-reduce | flops 1 | bytes 8 | tf_op jit(solution)/shard_map/psum | solution.py:192
  741.8 32.0 %while.70 = (s32[]{:T(128)}, f32[8,52]{1,0:T(8,128)S(1)}, s32[8,16384]{1,0:T(8,128)}, f32[8,16384]{1,0:T(8,128)}, s32[]{:T(128)}, /*index=5*/s32[]{:T(128)}) while((s32[]{:T(128)}, f32[8,52]{1,0:T(8,128)S(1)}, s32[8,16384]{1,0:T(8,128)}, f32[8,16384]{1,0:T(8,128)}, s32[]{:T(128)}, /*index=5*/s32[]{:T(128)}) %tuple.210), condition=%wide.region_21.22_spmd.clone, body=%wide.region_20.21_spmd.clone.sunk | while | flops 11075586 | bytes 263357 | solution.py:121
  742.9 2.9 fusion.176
  783.8 103.2 %all-gather.11.cloned.1.call-done = f32[256,1,5120]{2,1,0:T(1,128)} async-done(((f32[1,1,5120]{2,1,0:T(1,128)}), f32[256,1,5120]{2,1,0:T(1,128)}) %all-gather.11.cloned.1.call-update) | async-done | bytes 5242896 | tf_op jit(solution)/shard_map/all_gather | solution.py:174
  887.0 5.3 reduce_sum.117
  896.5 3.0 collective-permute-done.25
  900.4 34.7 %while.71 = (s32[]{:T(128)}, f32[8,16384]{1,0:T(8,128)}, s32[8,16384]{1,0:T(8,128)}, f32[52]{0:T(128)S(1)}, s32[]{:T(128)}, /*index=5*/s32[]{:T(128)}) while((s32[]{:T(128)}, f32[8,16384]{1,0:T(8,128)}, s32[8,16384]{1,0:T(8,128)}, f32[52]{0:T(128)S(1)}, s32[]{:T(128)}, /*index=5*/s32[]{:T(128)}) %tuple.207), condition=%wide.region_25.26_spmd.clone, body=%wide.region_24.25_spmd.clone.sunk | while | flops 11075586 | bytes 393501 | solution.py:130
  937.3 78.0 %psum.46 = f32[]{:T(128)} all-reduce(f32[]{:T(128)} %multiply_reduce_fusion.1), channel_id=1, replica_groups=mesh['gz'=32,'gy'=8] {'gz','gy'}, use_global_device_ids=true, to_apply=%region_27.28 | all-reduce | flops 1 | bytes 8 | tf_op jit(solution)/shard_map/psum | solution.py:182
  1019.8 4.0 collective-permute-start.27
  1025.2 3.7 collective-permute-start.28
  1034.5 76.0 %psum.47 = f32[]{:T(128)} all-reduce(f32[]{:T(128)} %get-tuple-element.282), channel_id=1, replica_groups=mesh['gz'=32,'gy'=8] {'gz','gy'}, use_global_device_ids=true, to_apply=%region_29.30 | all-reduce | flops 1 | bytes 8 | tf_op jit(solution)/shard_map/psum | solution.py:192
  (359 shorter events, 256.0 us)
Async XLA Ops:
  7.2 235.4 %copy-start = (f32[20,5120]{1,0:T(8,128)S(1)}, f32[20,5120]{1,0:T(8,128)}, u32[]{:S(2)}) copy-start(f32[20,5120]{1,0:T(8,128)} %param.21) | copy-start | bytes 1228804
  7.2 230.1 %all-gather.7.cloned.1.call-start = ((), (), s32[]{:S(2)}) async-start(), calls=%async_computation | async-start | bytes 5263360 | tf_op jit(solution)/shard_map/all_gather | solution.py:174
  8.2 5.7 collective-permute-start
  12.6 5.2 collective-permute-start.1
  17.9 6.9 collective-permute-start.2
  22.8 5.1 collective-permute-start.3
  30.2 7.2 collective-permute-start.4
  31.4 7.7 collective-permute-start.5
  39.9 8.7 collective-permute-start.6
  41.9 6.8 collective-permute-start.7
  54.2 6.5 collective-permute-start.8
  55.7 6.7 collective-permute-start.9
  62.4 6.9 collective-permute-start.10
  64.4 4.9 collective-permute-start.11
  68.2 43.3 %copy-start.33 = (pred[256]{0:T(512)(128)(4,1)}, pred[256]{0:T(512)(128)(4,1)S(1)}, u32[]{:S(2)}) copy-start(pred[256]{0:T(512)(128)(4,1)S(1)} %iota_compare_fusion.18) | copy-start | bytes 772
  79.1 33.8 %copy-start.3 = (f32[8,32,512]{2,1,0:T(8,128)S(1)}, f32[8,32,512]{2,1,0:T(8,128)}, u32[]{:S(2)}) copy-start(f32[8,32,512]{2,1,0:T(8,128)} %get-tuple-element.334) | copy-start | bytes 1572868
  112.4 411.3 %all-gather.9.cloned.1.call-start = ((), (), s32[]{:S(2)}) async-start(), calls=%async_computation.1 | async-start | bytes 5263360 | tf_op jit(solution)/shard_map/all_gather | solution.py:174
  115.5 297.8 %copy-start.16 = (f32[1,32,512]{2,1,0:T(8,128)}, f32[1,32,512]{2,1,0:T(8,128)S(1)}, u32[]{:S(2)}) copy-start(f32[1,32,512]{2,1,0:T(8,128)S(1)} %get-tuple-element.325) | copy-start | bytes 196612
  116.3 297.9 %copy-start.20 = (f32[1,32,512]{2,1,0:T(8,128)}, f32[1,32,512]{2,1,0:T(8,128)S(1)}, u32[]{:S(2)}) copy-start(f32[1,32,512]{2,1,0:T(8,128)S(1)} %get-tuple-element.316) | copy-start | bytes 196612
  116.3 297.9 %copy-start.21 = (f32[1,32,512]{2,1,0:T(8,128)}, f32[1,32,512]{2,1,0:T(8,128)S(1)}, u32[]{:S(2)}) copy-start(f32[1,32,512]{2,1,0:T(8,128)S(1)} %get-tuple-element.319) | copy-start | bytes 196612
  116.3 297.9 %copy-start.22 = (f32[1,32,512]{2,1,0:T(8,128)}, f32[1,32,512]{2,1,0:T(8,128)S(1)}, u32[]{:S(2)}) copy-start(f32[1,32,512]{2,1,0:T(8,128)S(1)} %get-tuple-element.320) | copy-start | bytes 196612
  116.3 298.0 %copy-start.23 = (f32[1,32,512]{2,1,0:T(8,128)}, f32[1,32,512]{2,1,0:T(8,128)S(1)}, u32[]{:S(2)}) copy-start(f32[1,32,512]{2,1,0:T(8,128)S(1)} %get-tuple-element.321) | copy-start | bytes 196612
  116.4 132.8 %copy-start.17 = (f32[8,32,512]{2,1,0:T(8,128)}, f32[8,32,512]{2,1,0:T(8,128)S(1)}, u32[]{:S(2)}) copy-start(f32[8,32,512]{2,1,0:T(8,128)S(1)} %constant_dynamic-update-slice_fusion.3) | copy-start | bytes 1572868
  243.2 5.3 collective-permute-start.13
  244.5 4.7 collective-permute-start.12
  274.9 5.5 collective-permute-start.14
  276.2 5.5 collective-permute-start.15
  281.7 7.5 collective-permute-start.16
  286.2 4.0 collective-permute-start.17
  379.7 32.4 %copy-start.34 = (pred[256]{0:T(512)(128)(4,1)S(1)}, pred[256]{0:T(512)(128)(4,1)}, u32[]{:S(2)}) copy-start(pred[256]{0:T(512)(128)(4,1)} %copy-done.33) | copy-start | bytes 772
  379.7 33.6 %copy-start.26 = (f32[1,32,512]{2,1,0:T(8,128)S(1)}, f32[1,32,512]{2,1,0:T(8,128)}, u32[]{:S(2)}) copy-start(f32[1,32,512]{2,1,0:T(8,128)} %get-tuple-element.330) | copy-start | bytes 196612
  379.7 34.6 %copy-start.24 = (f32[1,32,512]{2,1,0:T(8,128)S(1)}, f32[1,32,512]{2,1,0:T(8,128)}, u32[]{:S(2)}) copy-start(f32[1,32,512]{2,1,0:T(8,128)} %get-tuple-element.322) | copy-start | bytes 196612
  379.7 34.6 %copy-start.25 = (f32[1,32,512]{2,1,0:T(8,128)S(1)}, f32[1,32,512]{2,1,0:T(8,128)}, u32[]{:S(2)}) copy-start(f32[1,32,512]{2,1,0:T(8,128)} %get-tuple-element.323) | copy-start | bytes 196612
  413.0 473.9 %all-gather.11.cloned.1.call-start = ((), (), s32[]{:S(2)}) async-start(), calls=%async_computation.2 | async-start | bytes 5263360 | tf_op jit(solution)/shard_map/all_gather | solution.py:174
  529.6 3.6 collective-permute-start.18
  531.9 4.3 collective-permute-start.19
  559.5 80.5 %copy-start.12 = (f32[8,16384]{1,0:T(8,128)}, f32[8,16384]{1,0:T(8,128)S(1)}, u32[]{:S(2)}) copy-start(f32[8,16384]{1,0:T(8,128)S(1)} %get-tuple-element.167) | copy-start | bytes 1572868
  559.5 98.9 %copy-start.4 = (f32[8,32,512]{2,1,0:T(8,128)S(1)}, f32[8,32,512]{2,1,0:T(8,128)}, u32[]{:S(2)}) copy-start(f32[8,32,512]{2,1,0:T(8,128)} %get-tuple-element.334) | copy-start | bytes 1572868
  642.9 5.3 collective-permute-start.20
  644.2 5.3 collective-permute-start.21
  650.1 5.6 collective-permute-start.22
  653.8 3.3 collective-permute-start.23
  892.9 3.6 collective-permute-start.24
  895.2 4.3 collective-permute-start.25
  1018.5 5.3 collective-permute-start.26
  1019.8 5.3 collective-permute-start.27
  1025.2 5.6 collective-permute-start.28
  1028.9 3.1 collective-permute-start.29
  (21 other events, 238.1 us)
Sparse Core Ops, SparseCore 0:
  112.5 124.7 all-gather.6
  413.1 110.4 all-gather.8
  776.7 110.1 all-gather.10
